TPU v7x, 32 devices: a whole 2x2x4 slice. The times are simulated.
32 devices in a mesh: samp: 16 (over z, x, core), snp: 2 (over y).
Axes of the slice: x: 2, y: 2, z: 4, core: 2. Of those that a mesh axis runs over, the one named last changes fastest.
Arguments:
- genotype: int32 [10240, 4096], P('samp', 'snp'), may hold values from 0 to 2
- freqs: float32 [4096], P('snp'), may hold values from 0.35 to 0.65
- left_factors: float32 [10240, 20], P('samp'), may hold values from -6 to 6
- singular: float32 [20], replicated, may hold values from 0.5 to 2
- right_factors: float32 [4096, 20], P(('snp', 'samp')), may hold values from -1.25 to 1.25
- sketch: bfloat16 [4096, 64], P('snp'), may hold values from -6 to 6
- batch_sizes: int32 [12], replicated, may hold values from 1 to 1706, 10240 in all
- missing_batch: int32 [48], replicated, may hold values from 0 to 11, as said below
- missing_block: int32 [48], replicated, may hold values from 0 to 15, as said below
Outputs:
- basis: float32 [10240, 64], P('samp')
- projection: float32 [4096, 64], P('snp')
- snp_basis: float32 [4096, 64], P('snp')
Inputs may be any that keep to these rules, and one draw needn't show every extreme that they name: The pairs (missing_batch, missing_block) are distinct; every block id appears exactly 3 times and every batch id exactly 48 // 12 times. `missing_block`: paired entry by entry with missing_batch.
All inputs are finite; a program needn't handle non-finite values.
Results may differ from a plain program's by a relative error of at most 0.012.
Values may be sent and summed in bfloat16 or wider, within the bound.
A program may use at most 64 MiB of HBM per device.

v0:
```python
import math

import jax
import jax.numpy as jnp
from jax import lax
from jax.sharding import PartitionSpec as P

BATCHES = 12
BLOCK = 256
ITERS = 2
BLOCKS = 16


def finish_basis(values, gram):
    lower = jnp.linalg.cholesky(gram)
    return jax.scipy.linalg.solve_triangular(lower, values.T, lower=True).T


def reversed_basis(values, gram):
    flipped = finish_basis(values[:, ::-1], gram[::-1, ::-1])
    return flipped[:, ::-1]


def own_gram(values):
    return jnp.dot(values.T, values, precision=lax.Precision.HIGHEST)


def sample_basis(matrix, right_side, sample_count, is_last):
    partial_value = jnp.dot(matrix, right_side, preferred_element_type=jnp.float32)
    share = lax.psum_scatter(
        partial_value.astype(jnp.bfloat16), "snp", scatter_dimension=0, tiled=True
    ).astype(jnp.float32)
    gram = lax.psum(own_gram(share), ("samp", "snp")) / sample_count
    finished = finish_basis(share, gram)
    if is_last:
        return lax.all_gather(finished.astype(jnp.bfloat16), "snp", axis=0, tiled=True).astype(
            finished.dtype
        )
    return lax.all_gather(finished.astype(jnp.bfloat16), "snp", axis=0, tiled=True)


def snp_columns(matrix, basis):
    local_part = lax.dot_general(
        matrix,
        basis.astype(jnp.bfloat16),
        (((0,), (0,)), ((), ())),
        preferred_element_type=jnp.float32,
    )
    return lax.psum(local_part, "samp")


def snp_basis(columns, snp_count):
    gram = lax.psum(own_gram(columns), "snp") / snp_count
    return reversed_basis(columns, gram)


def on_device(
    genotype,
    freqs,
    left_factors,
    singular,
    right_factors,
    sketch,
    batch_sizes,
    missing_batch,
    missing_block,
):
    row_count, col_width = genotype.shape
    sample_count = row_count * lax.axis_size("samp")
    snp_count = col_width * lax.axis_size("snp")
    right_local = lax.all_gather(right_factors, "samp", axis=0, tiled=True)
    batch_range = jnp.arange(BATCHES, dtype=jnp.int32)
    block_range = jnp.arange(BLOCKS, dtype=jnp.int32)
    hot_batch = (missing_batch[:, None] == batch_range[None, :]).astype(jnp.float32)
    hot_block = (missing_block[:, None] == block_range[None, :]).astype(jnp.float32)
    table = jnp.dot(hot_batch.T, hot_block, preferred_element_type=jnp.float32)
    ends = jnp.cumsum(batch_sizes)
    row_ids = lax.axis_index("samp") * row_count + jnp.arange(row_count, dtype=jnp.int32)
    batch_of = jnp.sum((row_ids[:, None] >= ends[None, :]).astype(jnp.int32), axis=1)
    row_hot = (batch_of[:, None] == batch_range[None, :]).astype(jnp.float32)
    col_ids = lax.axis_index("snp") * col_width + jnp.arange(col_width, dtype=jnp.int32)
    col_hot = ((col_ids // BLOCK)[None, :] == block_range[:, None]).astype(jnp.float32)
    missing = (
        jnp.dot(
            jnp.dot(row_hot, table, preferred_element_type=jnp.float32),
            col_hot,
            preferred_element_type=jnp.float32,
        )
        > 0.5
    )
    lowrank = jnp.dot(
        left_factors * singular[None, :], right_local.T, precision=lax.Precision.HIGHEST
    )
    observed = genotype.astype(jnp.float32) - 2.0 * freqs[None, :]
    matrix = jnp.where(missing, lowrank, observed).astype(jnp.bfloat16)
    basis = sample_basis(matrix, sketch, sample_count, ITERS == 0)
    column_basis = jnp.zeros((col_width, sketch.shape[1]), jnp.float32)
    for sweep_index in range(ITERS):
        column_basis = snp_basis(snp_columns(matrix, basis), snp_count)
        basis = sample_basis(
            matrix, column_basis.astype(jnp.bfloat16), sample_count, sweep_index == ITERS - 1
        )
    projection = snp_columns(matrix, basis) / math.sqrt(sample_count)
    return (basis, projection, column_basis)


def solution(mesh):
    in_specs = (
        P("samp", "snp"),
        P("snp"),
        P("samp", None),
        P(),
        P(("snp", "samp"), None),
        P("snp", None),
        P(),
        P(),
        P(),
    )
    out_specs = (P("samp", None), P("snp", None), P("snp", None))
    return jax.shard_map(
        on_device, mesh=mesh, in_specs=in_specs, out_specs=out_specs, check_vma=False
    )
```

profile of v0, /device:TPU:0, one launch (start us, length us, event | category | flops | bytes accessed | tf_op | source)
XLA Modules:
  0.0 614.1 jit_solution(16106451307339280287)
XLA Ops:
  8.0 23.8 %all_gather.12 = f32[2048,20]{0,1:T(8,128)S(1)} all-gather(f32[128,20]{0,1:T(8,128)} %param.18), channel_id=1, replica_groups=mesh['samp'=16,'snp'=2] {'samp'}, dimensions={0}, use_global_device_ids=true | all-gather | bytes 174080 | tf_op jit(solution)/shard_map/all_gather | solution.py:71
  37.1 7.7 %select_convert_fusion = bf16[640,2048]{1,0:T(8,128)(2,1)S(1)} fusion(s32[640,2048]{1,0:T(8,128)} %param.14, f32[640,2048]{1,0:T(8,128)} %fusion.3, f32[2048,20]{0,1:T(8,128)S(1)} %all_gather.12, f32[2048]{0:T(1024)S(1)} %broadcast_multiply_fusion.6, f32[640,20]{0,1:T(8,128)S(1)} %copy-done.2, f32[20]{0:T(128)S(1)} %copy-done.3), kind=kOutput, calls=%fused_computation | convolution fusion | flops 321139200 | bytes 13330512 | tf_op jit(solution)/shard_map/dot_general | solution.py:91
  46.6 8.0 %reduce-scatter.10.cloned.1.call-done = bf16[320,64]{1,0:T(8,128)(2,1)} async-done(((bf16[640,64]{1,0:T(8,128)(2,1)}), bf16[320,64]{1,0:T(8,128)(2,1)}) %reduce-scatter.10.cloned.1.call-update) | async-done | bytes 40976
  55.8 39.5 %psum.56 = f32[64,64]{0,1:T(8,128)S(1)} all-reduce(f32[64,64]{0,1:T(8,128)S(1)} %fusion.50), channel_id=1, replica_groups=mesh['samp'=16,'snp'=2] {'samp','snp'}, use_global_device_ids=true, to_apply=%region_3.4 | all-reduce | flops 4096 | bytes 32768 | tf_op jit(solution)/shard_map/psum | solution.py:33
  95.4 5.8 cholesky.89
  115.5 90.6 %all-reduce.4.cloned.1.call-done = f32[2048,64]{0,1:T(8,128)} async-done(((f32[2048,64]{0,1:T(8,128)}), f32[2048,64]{0,1:T(8,128)}) %all-reduce.4.cloned.1.call-update) | async-done | bytes 524304 | tf_op jit(solution)/shard_map/psum | solution.py:49
  207.9 8.5 %psum.58 = f32[64,64]{0,1:T(8,128)S(1)} all-reduce(f32[64,64]{0,1:T(8,128)S(1)} %reverse.6), channel_id=1, replica_groups=mesh['samp'=16,'snp'=2] {'snp'}, use_global_device_ids=true, to_apply=%region_7.10 | all-reduce | flops 4096 | bytes 32768 | tf_op jit(solution)/shard_map/psum | solution.py:53
  216.5 5.8 cholesky.100
  228.6 6.1 rev.19
  236.1 5.9 rev.20
  243.8 10.3 %reduce-scatter.12.cloned.1.call-done = bf16[320,64]{1,0:T(8,128)(2,1)} async-done(((bf16[640,64]{1,0:T(8,128)(2,1)}), bf16[320,64]{1,0:T(8,128)(2,1)}) %reduce-scatter.12.cloned.1.call-update) | async-done | bytes 40976
  255.2 39.5 %psum.59 = f32[64,64]{0,1:T(8,128)S(1)} all-reduce(f32[64,64]{0,1:T(8,128)S(1)} %fusion.52), channel_id=1, replica_groups=mesh['samp'=16,'snp'=2] {'samp','snp'}, use_global_device_ids=true, to_apply=%region_9.13 | all-reduce | flops 4096 | bytes 32768 | tf_op jit(solution)/shard_map/psum | solution.py:33
  294.9 5.8 cholesky.111
  308.3 5.0 all-gather.1
  314.9 90.6 %all-reduce.6.cloned.1.call-done = f32[2048,64]{0,1:T(8,128)} async-done(((f32[2048,64]{0,1:T(8,128)}), f32[2048,64]{0,1:T(8,128)}) %all-reduce.6.cloned.1.call-update) | async-done | bytes 524304 | tf_op jit(solution)/shard_map/psum | solution.py:49
  407.4 8.3 %psum.61 = f32[64,64]{0,1:T(8,128)S(1)} all-reduce(f32[64,64]{0,1:T(8,128)S(1)} %reverse.7), channel_id=1, replica_groups=mesh['samp'=16,'snp'=2] {'snp'}, use_global_device_ids=true, to_apply=%region_11.15 | all-reduce | flops 4096 | bytes 32768 | tf_op jit(solution)/shard_map/psum | solution.py:53
  415.8 5.8 cholesky.122
  427.9 6.1 rev.22
  435.4 6.1 rev.23
  443.4 10.3 %reduce-scatter.14.cloned.1.call-done = bf16[320,64]{1,0:T(8,128)(2,1)} async-done(((bf16[640,64]{1,0:T(8,128)(2,1)}), bf16[320,64]{1,0:T(8,128)(2,1)}) %reduce-scatter.14.cloned.1.call-update) | async-done | bytes 40976
  454.8 39.7 %psum.62 = f32[64,64]{0,1:T(8,128)S(1)} all-reduce(f32[64,64]{0,1:T(8,128)S(1)} %fusion.54), channel_id=1, replica_groups=mesh['samp'=16,'snp'=2] {'samp','snp'}, use_global_device_ids=true, to_apply=%region_13.17 | all-reduce | flops 4096 | bytes 32768 | tf_op jit(solution)/shard_map/psum | solution.py:33
  494.7 5.8 cholesky.133
  508.0 5.0 all-gather.2
  515.4 90.0 %all-reduce.8.cloned.1.call-done = f32[2048,64]{0,1:T(8,128)} async-done(((f32[2048,64]{0,1:T(8,128)}), f32[2048,64]{0,1:T(8,128)}) %all-reduce.8.cloned.1.call-update) | async-done | bytes 524304 | tf_op jit(solution)/shard_map/psum | solution.py:49
  (95 shorter events, 69.2 us)
Async XLA Ops:
  7.2 37.6 %copy-start = (bf16[2048,64]{0,1:T(8,128)(2,1)S(1)}, bf16[2048,64]{0,1:T(8,128)(2,1)}, u32[]{:S(2)}) copy-start(bf16[2048,64]{0,1:T(8,128)(2,1)} %param.19) | copy-start | bytes 786436
  7.2 47.4 %reduce-scatter.10.cloned.1.call-start = ((), (), s32[]{:S(2)}) async-start(), calls=%async_computation.6 | async-start | bytes 245760
  33.6 3.4 copy-start.2
  33.6 3.4 copy-start.3
  46.5 159.5 %all-reduce.4.cloned.1.call-start = ((), (), s32[]{:S(2)}) async-start(), calls=%async_computation.3 | async-start | bytes 1048576 | tf_op jit(solution)/shard_map/psum | solution.py:49
  115.4 138.7 %reduce-scatter.12.cloned.1.call-start = ((), (), s32[]{:S(2)}) async-start(), calls=%async_computation.7 | async-start | bytes 245760
  243.7 161.8 %all-reduce.6.cloned.1.call-start = ((), (), s32[]{:S(2)}) async-start(), calls=%async_computation.4 | async-start | bytes 1048576 | tf_op jit(solution)/shard_map/psum | solution.py:49
  314.9 138.8 %reduce-scatter.14.cloned.1.call-start = ((), (), s32[]{:S(2)}) async-start(), calls=%async_computation.8 | async-start | bytes 245760
  441.6 1.8 copy-start.1
  443.3 162.0 %all-reduce.8.cloned.1.call-start = ((), (), s32[]{:S(2)}) async-start(), calls=%async_computation.5 | async-start | bytes 1048576 | tf_op jit(solution)/shard_map/psum | solution.py:49
Sparse Core Ops, SparseCore 0:
  46.7 7.9 reduce-scatter.9
  115.5 90.4 all-reduce.3
  243.9 10.1 reduce-scatter.11
  315.0 90.4 all-reduce.5
  443.4 10.1 reduce-scatter.13
  514.8 90.4 all-reduce.7
where the time goes:
time: 617 us; the launch traced here: 614 us
  waiting for transfers between devices  300 us (49%)
  blocking collectives  174 us (28%)
  other arithmetic  64.6 us (10%)
  local copies, waits for them, and re-layouts  30.9 us (5%)
  matrix products  29.6 us (5%)
  between operations  14.5 us (2%)
    psum x3, waiting for transfers between devices, snp_columns(): return lax.psum(local_part, 'samp')  271 us
    psum x3, blocking collectives, sample_basis(): gram = lax.psum(own_gram(share), ('samp', 'snp')) / sample_count  119 us
    another operation x15, other arithmetic, finish_basis(): lower = jnp.linalg.cholesky(gram)  32.6 us
    unnamed x9, waiting for transfers between devices  28.7 us
    another operation x10, other arithmetic, finish_basis(): return jax.scipy.linalg.solve_triangular(lower, values.T, lower=True).T  27.7 us
    all_gather x1, blocking collectives, on_device(): right_local = lax.all_gather(right_factors, 'samp', axis=0, tiled=True)  23.8 us
    psum x2, blocking collectives, snp_basis(): gram = lax.psum(own_gram(columns), 'snp') / snp_count  16.8 us
    all_gather x3, blocking collectives, sample_basis(): lax.all_gather(finished.astype(jnp.bfloat16), 'snp', axis=0, tiled=True)  15 us
  transfers between devices with their start and end apart: 6, of which 6 were waited for; matrix products, arithmetic and copies ran while one was open for 0% of the time, Pallas kernels for 0%

commit v1 on v0

v1 whole, which is shorter than its diff:
```python
import functools
import math

import jax
import jax.numpy as jnp
from jax import lax
from jax.experimental import pallas as pl
from jax.experimental.pallas import tpu as pltpu
from jax.sharding import PartitionSpec as P

BATCHES = 12
BLOCK = 256
ITERS = 2
MESH = pl.DeviceIdType.MESH
NT = (((1,), (1,)), ((), ()))
NN = (((1,), (0,)), ((), ()))
ROW_STEP = 128


def dot32(a, b):
    return lax.dot_general(
        a, b, NN, precision=lax.Precision.HIGHEST, preferred_element_type=jnp.float32
    )


def dot16(a, b, dims):
    return lax.dot_general(a, b, dims, preferred_element_type=jnp.float32)


def split2(v):
    hi = v.astype(jnp.bfloat16)
    lo = (v - hi.astype(jnp.float32)).astype(jnp.bfloat16)
    return hi, lo


def inverse_factor(gram, reverse):
    k = gram.shape[0]
    rows = lax.broadcasted_iota(jnp.int32, (k, 2 * k), 0)
    lanes = lax.broadcasted_iota(jnp.int32, (k, 2 * k), 1)
    row1 = lax.broadcasted_iota(jnp.int32, (k, 1), 0)
    unit = (lanes == rows + k).astype(jnp.float32)
    a = jnp.concatenate([gram, unit[:, k:]], axis=1)
    order = range(k - 1, 0, -1) if reverse else range(k - 1)
    for j in order:
        pivot = a[j : j + 1, j : j + 1]
        after = row1 < j if reverse else row1 > j
        factor = jnp.where(after, a[:, j : j + 1] * (1.0 / pivot), 0.0)
        a = a - factor * a[j : j + 1, :]
    diag = jnp.sum(jnp.where(lanes == rows, a, 0.0), axis=1, keepdims=True)
    return a[:, k:] * lax.rsqrt(diag)


def kernel(
    n,
    m,
    sample_count,
    snp_count,
    geno_ref,
    freqs_ref,
    lw_ref,
    right_ref,
    sketch_ref,
    mask_ref,
    basis_ref,
    proj_ref,
    snpb_ref,
    geno,
    x_ref,
    rg,
    rt,
    ysl,
    gsl,
    t_src,
    t_dst,
    gr_src,
    gr_dst,
    ga_src,
    ga_dst,
    gfull,
    zg,
    zt,
    geno_sem,
    rg_send,
    rg_recv,
    y_send,
    y_recv,
    gz_send,
    gz_recv,
    t_send,
    t_recv,
    gr_send,
    gr_recv,
    ga_send,
    ga_recv,
    z_send,
    z_recv,
):
    me = lax.axis_index("samp")
    my = lax.axis_index("snp")
    rows, cols = x_ref.shape
    k = sketch_ref.shape[1]
    width = cols // n
    steps = rows // ROW_STEP

    def geno_copy(i):
        at = pl.ds(i * ROW_STEP, ROW_STEP)
        return pltpu.make_async_copy(geno_ref.at[at], geno.at[at], geno_sem.at[i])

    for i in range(steps):
        geno_copy(i).start()

    barrier = pltpu.get_barrier_semaphore()

    def greet_samp(o, c):
        pl.semaphore_signal(
            barrier, inc=1, device_id={"samp": lax.rem(me + o, n)}, device_id_type=MESH
        )
        return c

    def greet_snp(o, c):
        pl.semaphore_signal(
            barrier, inc=1, device_id={"snp": lax.rem(my + o, m)}, device_id_type=MESH
        )
        return c

    lax.fori_loop(1, n, greet_samp, 0)
    lax.fori_loop(1, m, greet_snp, 0)
    pl.semaphore_wait(barrier, n + m - 2)

    def remote(src, dst, send, recv, axis, peer):
        return pltpu.make_async_remote_copy(
            src_ref=src,
            dst_ref=dst,
            send_sem=send,
            recv_sem=recv,
            device_id={axis: peer},
            device_id_type=MESH,
        )

    def start_all(axis, size, mine, src_of, dst, send, recv):
        def body(o, c):
            peer = lax.rem(mine + o, size)
            remote(src_of(peer), dst.at[mine], send.at[o], recv.at[o], axis, peer).start()
            return c

        lax.fori_loop(1, size, body, 0)

    def wait_all(axis, size, mine, src_of, dst, send, recv):
        def body(o, c):
            peer = lax.rem(mine + o, size)
            source = lax.rem(mine + size - o, size)
            remote(src_of(peer), dst.at[source], send.at[o], recv.at[o], axis, peer).wait()
            return c

        lax.fori_loop(1, size, body, 0)

    def one(ref):
        return lambda peer: ref

    def per_peer(ref):
        return lambda peer: ref.at[peer]

    rg_args = ("samp", n, me, one(right_ref), rg, rg_send, rg_recv)
    start_all(*rg_args)
    rg[me] = right_ref[...]
    sketch_t = sketch_ref[...].astype(jnp.float32).T.astype(jnp.bfloat16)
    wait_all(*rg_args)
    depth = right_ref.shape[0]
    for p in range(n):
        piece = rg[p]
        b1 = piece.astype(jnp.bfloat16)
        r1 = piece - b1.astype(jnp.float32)
        b2 = r1.astype(jnp.bfloat16)
        b3 = (r1 - b2.astype(jnp.float32)).astype(jnp.bfloat16)
        for i, part in enumerate((b1, b2, b1, b3, b2, b1)):
            rt[i * depth : (i + 1) * depth, p * width : (p + 1) * width] = part

    def build(i, c):
        geno_copy(i).wait()
        at = pl.ds(pl.multiple_of(i * ROW_STEP, ROW_STEP), ROW_STEP)
        for b in range(cols // BLOCK):
            cut = slice(b * BLOCK, (b + 1) * BLOCK)
            lowrank = dot16(lw_ref[at, :], rt[:, cut], NN)
            observed = geno[at, cut].astype(jnp.float32) - 2.0 * freqs_ref[:, cut]
            gone = mask_ref[at, b : b + 1] > 0.5
            x_ref[at, cut] = jnp.where(gone, lowrank, observed).astype(jnp.bfloat16)
        return c

    lax.fori_loop(0, steps, build, 0)

    def snp_sum(value, slots, send, recv):
        slots[my] = value
        args = ("snp", m, my, one(slots.at[my]), slots, send, recv)
        start_all(*args)

        def finish():
            wait_all(*args)
            total = slots[0]
            for q in range(1, m):
                total = total + slots[q]
            return total

        return finish

    y = snp_sum(dot16(sketch_t, x_ref[...], NT), ysl.at[0], y_send.at[0], y_recv.at[0])()
    piece_rows = k // n
    for it in range(ITERS + 1):
        hi, lo = split2(y)
        both = jnp.concatenate([hi, lo], axis=0)
        g4 = dot16(both, both, NT)
        gram = g4[:k, :k] + (g4[:k, k:] + g4[k:, :k])
        for p in range(n):
            gr_src[it, p] = gram[p * piece_rows : (p + 1) * piece_rows]
        gr_args = ("samp", n, me, per_peer(gr_src.at[it]), gr_dst.at[it], gr_send.at[it], gr_recv.at[it])
        start_all(*gr_args)

        t2 = dot16(both, x_ref[...], NN)
        t = t2[:k] + t2[k:]
        for p in range(n):
            t_src[it, p] = t[:, p * width : (p + 1) * width]
        t_args = ("samp", n, me, per_peer(t_src.at[it]), t_dst.at[it], t_send.at[it], t_recv.at[it])
        start_all(*t_args)

        wait_all(*gr_args)
        gr_dst[it, me] = gr_src[it, me]
        piece = gr_dst[it, 0]
        for p in range(1, n):
            piece = piece + gr_dst[it, p]
        ga_src[it] = piece
        ga_args = ("samp", n, me, one(ga_src.at[it]), ga_dst.at[it], ga_send.at[it], ga_recv.at[it])
        start_all(*ga_args)
        ga_dst[it, me] = piece
        if it == ITERS:
            snpb_ref[...] = dot32(upper, zt[...].astype(jnp.float32))
        wait_all(*ga_args)
        for p in range(n):
            gfull[p * piece_rows : (p + 1) * piece_rows, :] = ga_dst[it, p]
        lower = inverse_factor(gfull[...] * (1.0 / sample_count), False)

        wait_all(*t_args)
        t_dst[it, me] = t_src[it, me]
        chunk = t_dst[it, 0]
        for p in range(1, n):
            chunk = chunk + t_dst[it, p]
        z = dot32(lower, chunk)
        if it == ITERS:
            z = z * (1.0 / math.sqrt(sample_count))
        zg[it, me] = z.astype(jnp.bfloat16)
        z_args = ("samp", n, me, one(zg.at[it, me]), zg.at[it], z_send.at[it], z_recv.at[it])
        start_all(*z_args)
        if it == ITERS:
            basis_ref[...] = dot32(lower, y)
            wait_all(*z_args)
            for p in range(n):
                proj_ref[:, p * width : (p + 1) * width] = zg[it, p].astype(jnp.float32)
            return
        wait_all(*z_args)
        for p in range(n):
            zt[:, p * width : (p + 1) * width] = zg[it, p]
        zz = zt[...]
        gz_done = snp_sum(dot16(zz, zz, NT), gsl.at[it], gz_send.at[it], gz_recv.at[it])
        v_done = snp_sum(
            dot16(zz, x_ref[...], NT), ysl.at[it + 1], y_send.at[it + 1], y_recv.at[it + 1]
        )
        upper = inverse_factor(gz_done() * (1.0 / snp_count), True)
        y = dot32(upper, v_done())


def on_device(
    n,
    m,
    genotype,
    freqs,
    left_factors,
    singular,
    right_factors,
    sketch,
    batch_sizes,
    missing_batch,
    missing_block,
):
    rows, cols = genotype.shape
    k = sketch.shape[1]
    rank = left_factors.shape[1]
    depth = -(-rank // 32) * 32
    width = cols // n
    batch_range = jnp.arange(BATCHES, dtype=jnp.int32)
    upto = batch_range[:, None] >= batch_range[None, :]
    ends = jnp.sum(jnp.where(upto, batch_sizes[None, :], 0), axis=1)
    begins = ends - batch_sizes
    hot = missing_batch[:, None] == batch_range[None, :]
    first = jnp.sum(jnp.where(hot, begins[None, :], 0), axis=1)
    last = jnp.sum(jnp.where(hot, ends[None, :], 0), axis=1)
    row_ids = lax.axis_index("samp") * rows + jnp.arange(rows, dtype=jnp.int32)
    inside = (row_ids[:, None] >= first[None, :]) & (row_ids[:, None] < last[None, :])
    local_block = missing_block - lax.axis_index("snp") * (cols // BLOCK)
    hot_block = local_block[:, None] == jnp.arange(128, dtype=jnp.int32)[None, :]
    mask = jnp.dot(
        inside.astype(jnp.bfloat16),
        hot_block.astype(jnp.bfloat16),
        preferred_element_type=jnp.float32,
    )

    weighted = jnp.pad(left_factors * singular[None, :], ((0, 0), (0, depth - rank)))
    a1 = lax.reduce_precision(weighted, 8, 7)
    a2 = lax.reduce_precision(weighted - a1, 8, 7)
    a3 = lax.reduce_precision(weighted - a1 - a2, 8, 7)
    lw = jnp.concatenate([a1, a1, a2, a1, a2, a3], axis=1).astype(jnp.bfloat16)
    right_t = jnp.pad(right_factors.T, ((0, depth - rank), (0, 0)))

    f32, b16 = jnp.float32, jnp.bfloat16
    vm = pl.BlockSpec(memory_space=pltpu.VMEM)
    dma = pltpu.SemaphoreType.DMA
    loops = ITERS + 1
    piece = k // n
    basis_t, proj_t, snpb_t = pl.pallas_call(
        functools.partial(
            kernel,
            n,
            m,
            float(rows * n),
            float(cols * m),
        ),
        out_shape=(
            jax.ShapeDtypeStruct((k, rows), f32),
            jax.ShapeDtypeStruct((k, cols), f32),
            jax.ShapeDtypeStruct((k, cols), f32),
        ),
        in_specs=[pl.BlockSpec(memory_space=pl.ANY)] + [vm] * 5,
        out_specs=(vm, vm, vm),
        scratch_shapes=[
            pltpu.VMEM((rows, cols), jnp.int32),
            pltpu.VMEM((rows, cols), b16),
            pltpu.VMEM((n, depth, width), f32),
            pltpu.VMEM((6 * depth, cols), b16),
            pltpu.VMEM((loops, m, k, rows), f32),
            pltpu.VMEM((ITERS, m, k, k), f32),
            pltpu.VMEM((loops, n, k, width), f32),
            pltpu.VMEM((loops, n, k, width), f32),
            pltpu.VMEM((loops, n, piece, k), f32),
            pltpu.VMEM((loops, n, piece, k), f32),
            pltpu.VMEM((loops, piece, k), f32),
            pltpu.VMEM((loops, n, piece, k), f32),
            pltpu.VMEM((k, k), f32),
            pltpu.VMEM((loops, n, k, width), b16),
            pltpu.VMEM((k, cols), b16),
            dma((rows // ROW_STEP,)),
            dma((n,)),
            dma((n,)),
            dma((loops, m)),
            dma((loops, m)),
            dma((ITERS, m)),
            dma((ITERS, m)),
            dma((loops, n)),
            dma((loops, n)),
            dma((loops, n)),
            dma((loops, n)),
            dma((loops, n)),
            dma((loops, n)),
            dma((loops, n)),
            dma((loops, n)),
        ],
        compiler_params=pltpu.CompilerParams(
            collective_id=0, has_side_effects=True, vmem_limit_bytes=48 * 1024 * 1024
        ),
        cost_estimate=pl.CostEstimate(
            flops=12 * rows * cols * k, bytes_accessed=4 * rows * cols, transcendentals=0
        ),
    )(genotype, freqs[None, :], lw, right_t, sketch, mask)
    return basis_t.T, proj_t.T, snpb_t.T


def solution(mesh):
    in_specs = (
        P("samp", "snp"),
        P("snp"),
        P("samp", None),
        P(),
        P(("snp", "samp"), None),
        P("snp", None),
        P(),
        P(),
        P(),
    )
    out_specs = (P("samp", None), P("snp", None), P("snp", None))
    body = functools.partial(on_device, mesh.shape["samp"], mesh.shape["snp"])
    return jax.shard_map(
        body, mesh=mesh, in_specs=in_specs, out_specs=out_specs, check_vma=False
    )
```

time: 617 us -> 138 us (0.22)
  waiting for transfers between devices: 300 us -> 0 us
  blocking collectives: 174 us -> 0 us
  Pallas kernels: 0 us -> 126 us
  other arithmetic: 64.6 us -> 3.61 us
  matrix products: 29.6 us -> 0.28 us
  local copies, waits for them, and re-layouts: 30.9 us -> 6.35 us
  between operations: 14.5 us -> 0.69 us
    psum x3 -> x0, waiting for transfers between devices: 271 us -> none  [snp_columns(): return lax.psum(local_part, 'samp')]
    psum x5 -> x0, blocking collectives: 136 us -> none  [the longest x3 119 us: sample_basis(): gram = lax.psum(own_gram(share), ('samp', 'snp')) / sample_count]
    pallas_call x0 -> x1, Pallas kernels: none -> 126 us  [on_device(): pl.pallas_call(functools.partial(kernel, n, m, float(rows * n), float(col...]
    another operation x26 -> x1, other arithmetic: 61.2 us -> 0.09 us  [the longest x15 32.6 us: finish_basis(): lower = jnp.linalg.cholesky(gram)]
    all_gather x4 -> x0, blocking collectives: 38.8 us -> none  [the longest x1 23.8 us: on_device(): right_local = lax.all_gather(right_factors, 'samp', axis=0, tiled=True)]
    unnamed x9 -> x0, waiting for transfers between devices: 28.7 us -> none
    dot_general x14 -> x1, matrix products: 25.9 us -> 0.28 us  [on_device(): jnp.dot(inside.astype(jnp.bfloat16), hot_block.astype(jnp.bfloat16), pref...]
    rev x6 -> x0, local copies, waits for them, and re-layouts: 24.4 us -> none  [the longest x4 12.4 us: reversed_basis(): flipped = finish_basis(values[:, ::-1], gram[::-1, ::-1])]
  transfers between devices with their start and end apart: 6 -> 0, of which waited for: 6 -> 0; matrix products, arithmetic and copies ran while one was open for 0% -> 0% of each run, Pallas kernels for 0% -> 0%
where the time goes in v1:
time: 138 us; the launch traced here: 136 us
  Pallas kernels  126 us (91%)
  local copies, waits for them, and re-layouts  6.35 us (5%)
  other arithmetic  3.61 us (3%)
    pallas_call x1, Pallas kernels, on_device(): pl.pallas_call(functools.partial(kernel, n, m, float(rows * n), float(col...  126 us
    unnamed x7, local copies, waits for them, and re-layouts  5.17 us

profile of v1, /device:TPU:0, one launch (start us, length us, event | category | flops | bytes accessed | tf_op | source)
XLA Modules:
  0.0 136.5 jit_solution(14124599839356883081)
XLA Ops:
  0.6 0.7 broadcast_subtract_fusion
  1.3 0.8 select_reduce_fusion.2
  2.1 0.7 sub.18
  2.7 0.7 select_reduce_fusion.1
  3.5 0.7 pad.9.right_ref
  4.2 0.3 fusion.2.mask_ref
  4.5 1.0 copy.16
  5.5 0.7 broadcast_multiply_fusion
  6.2 0.1 fusion.1
  6.3 0.5 concatenate.4.lw_ref
  6.7 1.2 copy.18.sketch_ref
  8.0 0.0 copy-start
  8.0 0.7 copy-done
  8.7 125.5 %shard_map.112 = (f32[64,640]{1,0:T(8,128)S(1)}, f32[64,2048]{1,0:T(8,128)S(1)}, f32[64,2048]{1,0:T(8,128)S(1)}) custom-call(s32[640,2048]{1,0:T(8,128)} %geno_ref.1, f32[1,2048]{1,0:T(1,128)S(1)} %bitcast.8, bf16[640,192]{1,0:T(8,128)(2,1)S(1)} %concatenate.4.lw_ref, f32[32,128]{1,0:T(8,128)S(1)} %pad.9.right_ref, bf16[2048,64]{1,0:T(8,128)(2,1)S(1)} %copy.18.sketch_ref, ...), custom_call_target="tpu_custom_call" | custom-call | flops 1006632960 | bytes 5242880 | tf_op jit(solution)/shard_map/pallas_call | solution.py:316
  134.2 0.7 copy.22
  134.9 0.8 copy.23
  135.7 0.8 copy.24
  (1 shorter events, 0.0 us)
Async XLA Ops:
  8.0 0.7 copy-start

commit v2 on v1

--- a/solution.py
+++ b/solution.py
@@ -15,6 +15,7 @@
 NT = (((1,), (1,)), ((), ()))
 NN = (((1,), (0,)), ((), ()))
 ROW_STEP = 128
+GROUP = 8
 
 
 def dot32(a, b):
@@ -37,15 +38,34 @@
     k = gram.shape[0]
     rows = lax.broadcasted_iota(jnp.int32, (k, 2 * k), 0)
     lanes = lax.broadcasted_iota(jnp.int32, (k, 2 * k), 1)
-    row1 = lax.broadcasted_iota(jnp.int32, (k, 1), 0)
     unit = (lanes == rows + k).astype(jnp.float32)
     a = jnp.concatenate([gram, unit[:, k:]], axis=1)
-    order = range(k - 1, 0, -1) if reverse else range(k - 1)
-    for j in order:
-        pivot = a[j : j + 1, j : j + 1]
-        after = row1 < j if reverse else row1 > j
-        factor = jnp.where(after, a[:, j : j + 1] * (1.0 / pivot), 0.0)
-        a = a - factor * a[j : j + 1, :]
+    done = []
+    for step in range(0, k, GROUP):
+        count = a.shape[0]
+        base = 0 if reverse else step
+        local = lax.broadcasted_iota(jnp.int32, (count, 2 * k), 0)
+        if reverse:
+            group = [count - 1 - i for i in range(GROUP)]
+        else:
+            group = list(range(GROUP))
+        columns = [
+            jnp.broadcast_to(a[:, base + j : base + j + 1], (count, 2 * k)) for j in group
+        ]
+        for i, j in enumerate(group):
+            after = local < j if reverse else local > j
+            scale = 1.0 / columns[i][j : j + 1, :]
+            factor = jnp.where(after, columns[i] * scale, 0.0)
+            for later in range(i + 1, GROUP):
+                columns[later] = columns[later] - factor * columns[later][j : j + 1, :]
+            a = a - factor * a[j : j + 1, :]
+        if reverse:
+            done.insert(0, a[count - GROUP :])
+            a = a[: count - GROUP]
+        else:
+            done.append(a[:GROUP])
+            a = a[GROUP:]
+    a = jnp.concatenate(done, axis=0)
     diag = jnp.sum(jnp.where(lanes == rows, a, 0.0), axis=1, keepdims=True)
     return a[:, k:] * lax.rsqrt(diag)
 
@@ -71,6 +91,8 @@
     ysl,
     gsl,
     t_src,
+    t_half,
+    t_sum,
     t_dst,
     gr_src,
     gr_dst,
@@ -86,8 +108,12 @@
     y_recv,
     gz_send,
     gz_recv,
+    h_send,
+    h_recv,
     t_send,
     t_recv,
+    zh_send,
+    zh_recv,
     gr_send,
     gr_recv,
     ga_send,
@@ -101,6 +127,14 @@
     k = sketch_ref.shape[1]
     width = cols // n
     steps = rows // ROW_STEP
+    chips = n // 2
+    half = cols // 2
+    core = lax.rem(me, 2)
+    chip = me // 2
+    sibling = me + 1 - 2 * core
+
+    def half_of(which):
+        return pl.ds(pl.multiple_of(which * half, half), half)
 
     def geno_copy(i):
         at = pl.ds(i * ROW_STEP, ROW_STEP)
@@ -153,6 +187,23 @@
             return c
 
         lax.fori_loop(1, size, body, 0)
+
+    def start_chips(src_of, dst, send, recv):
+        def body(o, c):
+            to = lax.rem(chip + o, chips)
+            remote(src_of(to), dst.at[chip], send.at[o], recv.at[o], "samp", 2 * to + core).start()
+            return c
+
+        lax.fori_loop(1, chips, body, 0)
+
+    def wait_chips(src_of, dst, send, recv):
+        def body(o, c):
+            to = lax.rem(chip + o, chips)
+            source = lax.rem(chip + chips - o, chips)
+            remote(src_of(to), dst.at[source], send.at[o], recv.at[o], "samp", 2 * to + core).wait()
+            return c
+
+        lax.fori_loop(1, chips, body, 0)
 
     def one(ref):
         return lambda peer: ref
@@ -214,12 +265,23 @@
         gr_args = ("samp", n, me, per_peer(gr_src.at[it]), gr_dst.at[it], gr_send.at[it], gr_recv.at[it])
         start_all(*gr_args)
 
-        t2 = dot16(both, x_ref[...], NN)
-        t = t2[:k] + t2[k:]
-        for p in range(n):
+        def sketch_half(which):
+            t2 = dot16(both, x_ref[:, half_of(which)], NN)
+            return t2[:k] + t2[k:]
+
+        t = sketch_half(1 - core)
+        for p in range(chips):
             t_src[it, p] = t[:, p * width : (p + 1) * width]
-        t_args = ("samp", n, me, per_peer(t_src.at[it]), t_dst.at[it], t_send.at[it], t_recv.at[it])
-        start_all(*t_args)
+        across = remote(
+            t_src.at[it], t_half.at[it], h_send.at[it], h_recv.at[it], "samp", sibling
+        )
+        across.start()
+        t = sketch_half(core)
+        across.wait()
+        for p in range(chips):
+            t_sum[it, p] = t[:, p * width : (p + 1) * width] + t_half[it, p]
+        t_args = (per_peer(t_sum.at[it]), t_dst.at[it], t_send.at[it], t_recv.at[it])
+        start_chips(*t_args)
 
         wait_all(*gr_args)
         gr_dst[it, me] = gr_src[it, me]
@@ -231,37 +293,53 @@
         start_all(*ga_args)
         ga_dst[it, me] = piece
         if it == ITERS:
-            snpb_ref[...] = dot32(upper, zt[...].astype(jnp.float32))
+            for c in range(2):
+                snpb_ref[:, c * half : (c + 1) * half] = dot32(upper, zt[c].astype(jnp.float32))
         wait_all(*ga_args)
         for p in range(n):
             gfull[p * piece_rows : (p + 1) * piece_rows, :] = ga_dst[it, p]
         lower = inverse_factor(gfull[...] * (1.0 / sample_count), False)
 
-        wait_all(*t_args)
-        t_dst[it, me] = t_src[it, me]
+        wait_chips(*t_args)
+        t_dst[it, chip] = t_sum[it, chip]
         chunk = t_dst[it, 0]
-        for p in range(1, n):
+        for p in range(1, chips):
             chunk = chunk + t_dst[it, p]
         z = dot32(lower, chunk)
         if it == ITERS:
             z = z * (1.0 / math.sqrt(sample_count))
-        zg[it, me] = z.astype(jnp.bfloat16)
-        z_args = ("samp", n, me, one(zg.at[it, me]), zg.at[it], z_send.at[it], z_recv.at[it])
-        start_all(*z_args)
+        zg[it, core, chip] = z.astype(jnp.bfloat16)
+        z_args = (one(zg.at[it, core, chip]), zg.at[it, core], z_send.at[it], z_recv.at[it])
+        start_chips(*z_args)
         if it == ITERS:
             basis_ref[...] = dot32(lower, y)
-            wait_all(*z_args)
-            for p in range(n):
-                proj_ref[:, p * width : (p + 1) * width] = zg[it, p].astype(jnp.float32)
+        wait_chips(*z_args)
+        across = remote(
+            zg.at[it, core], zg.at[it, core], zh_send.at[it], zh_recv.at[it], "samp", sibling
+        )
+        across.start()
+        landed = remote(
+            zg.at[it, core], zg.at[it, 1 - core], zh_send.at[it], zh_recv.at[it], "samp", sibling
+        )
+        if it == ITERS:
+            landed.wait()
+            for c in range(2):
+                for p in range(chips):
+                    at = c * half + p * width
+                    proj_ref[:, at : at + width] = zg[it, c, p].astype(jnp.float32)
             return
-        wait_all(*z_args)
-        for p in range(n):
-            zt[:, p * width : (p + 1) * width] = zg[it, p]
-        zz = zt[...]
-        gz_done = snp_sum(dot16(zz, zz, NT), gsl.at[it], gz_send.at[it], gz_recv.at[it])
-        v_done = snp_sum(
-            dot16(zz, x_ref[...], NT), ysl.at[it + 1], y_send.at[it + 1], y_recv.at[it + 1]
-        )
+
+        def use_half(which):
+            for p in range(chips):
+                zt[which, :, p * width : (p + 1) * width] = zg[it, which, p]
+            zz = zt[which]
+            return dot16(zz, zz, NT), dot16(zz, x_ref[:, half_of(which)], NT)
+
+        gz_own, v_own = use_half(core)
+        landed.wait()
+        gz_far, v_far = use_half(1 - core)
+        gz_done = snp_sum(gz_own + gz_far, gsl.at[it], gz_send.at[it], gz_recv.at[it])
+        v_done = snp_sum(v_own + v_far, ysl.at[it + 1], y_send.at[it + 1], y_recv.at[it + 1])
         upper = inverse_factor(gz_done() * (1.0 / snp_count), True)
         y = dot32(upper, v_done())
 
@@ -335,15 +413,17 @@
             pltpu.VMEM((6 * depth, cols), b16),
             pltpu.VMEM((loops, m, k, rows), f32),
             pltpu.VMEM((ITERS, m, k, k), f32),
-            pltpu.VMEM((loops, n, k, width), f32),
-            pltpu.VMEM((loops, n, k, width), f32),
+            pltpu.VMEM((loops, n // 2, k, width), f32),
+            pltpu.VMEM((loops, n // 2, k, width), f32),
+            pltpu.VMEM((loops, n // 2, k, width), f32),
+            pltpu.VMEM((loops, n // 2, k, width), f32),
             pltpu.VMEM((loops, n, piece, k), f32),
             pltpu.VMEM((loops, n, piece, k), f32),
             pltpu.VMEM((loops, piece, k), f32),
             pltpu.VMEM((loops, n, piece, k), f32),
             pltpu.VMEM((k, k), f32),
-            pltpu.VMEM((loops, n, k, width), b16),
-            pltpu.VMEM((k, cols), b16),
+            pltpu.VMEM((loops, 2, n // 2, k, width), b16),
+            pltpu.VMEM((2, k, cols // 2), b16),
             dma((rows // ROW_STEP,)),
             dma((n,)),
             dma((n,)),
@@ -351,14 +431,18 @@
             dma((loops, m)),
             dma((ITERS, m)),
             dma((ITERS, m)),
+            dma((loops,)),
+            dma((loops,)),
+            dma((loops, n // 2)),
+            dma((loops, n // 2)),
+            dma((loops,)),
+            dma((loops,)),
             dma((loops, n)),
             dma((loops, n)),
             dma((loops, n)),
             dma((loops, n)),
-            dma((loops, n)),
-            dma((loops, n)),
-            dma((loops, n)),
-            dma((loops, n)),
+            dma((loops, n // 2)),
+            dma((loops, n // 2)),
         ],
         compiler_params=pltpu.CompilerParams(
             collective_id=0, has_side_effects=True, vmem_limit_bytes=48 * 1024 * 1024

time: 138 us -> 109 us (0.79)
  Pallas kernels: 126 us -> 97.3 us
    pallas_call x1, Pallas kernels: 126 us -> 97.3 us  [on_device(): pl.pallas_call(functools.partial(kernel, n, m, float(rows * n), float(col...]
where the time goes in v2:
time: 109 us; the launch traced here: 108 us
  Pallas kernels  97.3 us (89%)
  local copies, waits for them, and re-layouts  6.35 us (6%)
  other arithmetic  3.61 us (3%)
    pallas_call x1, Pallas kernels, on_device(): pl.pallas_call(functools.partial(kernel, n, m, float(rows * n), float(col...  97.3 us
    unnamed x7, local copies, waits for them, and re-layouts  5.17 us

profile of v2, /device:TPU:0, one launch (start us, length us, event | category | flops | bytes accessed | tf_op | source)
XLA Modules:
  0.0 108.2 jit_solution(2069140634233418233)
XLA Ops:
  0.6 0.7 broadcast_subtract_fusion
  1.3 0.8 select_reduce_fusion.2
  2.1 0.7 sub.18
  2.7 0.7 select_reduce_fusion.1
  3.5 0.7 pad.9.right_ref
  4.2 0.3 fusion.2.mask_ref
  4.5 1.0 copy.16
  5.5 0.7 broadcast_multiply_fusion
  6.2 0.1 fusion.1
  6.3 0.5 concatenate.4.lw_ref
  6.7 1.2 %copy.18.sketch_ref = bf16[2048,64]{1,0:T(8,128)(2,1)S(1)} copy(bf16[2048,64]{0,1:T(8,128)(2,1)} %param.14) | data formatting | bytes 524288 | tf_op args[5]
  8.0 0.0 copy-start
  8.0 0.7 copy-done
  8.7 97.3 %shard_map.112 = (f32[64,640]{1,0:T(8,128)S(1)}, f32[64,2048]{1,0:T(8,128)S(1)}, f32[64,2048]{1,0:T(8,128)S(1)}) custom-call(s32[640,2048]{1,0:T(8,128)} %geno_ref.1, f32[1,2048]{1,0:T(1,128)S(1)} %bitcast.8, bf16[640,192]{1,0:T(8,128)(2,1)S(1)} %concatenate.4.lw_ref, f32[32,128]{1,0:T(8,128)S(1)} %pad.9.right_ref, bf16[2048,64]{1,0:T(8,128)(2,1)S(1)} %copy.18.sketch_ref, ...), custom_call_target="tpu_custom_call" | custom-call | flops 1006632960 | bytes 5242880 | tf_op jit(solution)/shard_map/pallas_call | solution.py:394
  105.9 0.7 copy.22
  106.6 0.8 copy.23
  107.4 0.8 copy.24
  (1 shorter events, 0.0 us)
Async XLA Ops:
  8.0 0.7 copy-start

commit v3 on v2

--- a/solution.py
+++ b/solution.py
@@ -88,12 +88,15 @@
     x_ref,
     rg,
     rt,
+    yfirst,
     ysl,
     gsl,
     t_src,
     t_half,
     t_sum,
     t_dst,
+    t_sum16,
+    t_dst16,
     gr_src,
     gr_dst,
     ga_src,
@@ -104,6 +107,8 @@
     geno_sem,
     rg_send,
     rg_recv,
+    rh_send,
+    rh_recv,
     y_send,
     y_recv,
     gz_send,
@@ -211,14 +216,18 @@
     def per_peer(ref):
         return lambda peer: ref.at[peer]
 
-    rg_args = ("samp", n, me, one(right_ref), rg, rg_send, rg_recv)
-    start_all(*rg_args)
-    rg[me] = right_ref[...]
-    sketch_t = sketch_ref[...].astype(jnp.float32).T.astype(jnp.bfloat16)
-    wait_all(*rg_args)
-    depth = right_ref.shape[0]
+    rg_args = (one(right_ref), rg.at[core], rg_send, rg_recv)
+    start_chips(*rg_args)
+    rg[core, chip] = right_ref[...]
+    depth = rt.shape[0] // 6
+    wait_chips(*rg_args)
+    across = remote(rg.at[core], rg.at[core], rh_send, rh_recv, "samp", sibling)
+    across.start()
+    landed = remote(rg.at[core], rg.at[1 - core], rh_send, rh_recv, "samp", sibling)
+    landed.wait()
+    blank = jnp.zeros((depth - right_ref.shape[0], width), jnp.float32)
     for p in range(n):
-        piece = rg[p]
+        piece = jnp.concatenate([rg[p % 2, p // 2], blank], axis=0)
         b1 = piece.astype(jnp.bfloat16)
         r1 = piece - b1.astype(jnp.float32)
         b2 = r1.astype(jnp.bfloat16)
@@ -246,14 +255,15 @@
 
         def finish():
             wait_all(*args)
-            total = slots[0]
+            total = slots[0].astype(jnp.float32)
             for q in range(1, m):
-                total = total + slots[q]
+                total = total + slots[q].astype(jnp.float32)
             return total
 
         return finish
 
-    y = snp_sum(dot16(sketch_t, x_ref[...], NT), ysl.at[0], y_send.at[0], y_recv.at[0])()
+    first = dot16(x_ref[...], sketch_ref[...], NN).T.astype(jnp.bfloat16)
+    y = snp_sum(first, yfirst, y_send.at[0], y_recv.at[0])()
     piece_rows = k // n
     for it in range(ITERS + 1):
         hi, lo = split2(y)
@@ -279,8 +289,14 @@
         t = sketch_half(core)
         across.wait()
         for p in range(chips):
-            t_sum[it, p] = t[:, p * width : (p + 1) * width] + t_half[it, p]
-        t_args = (per_peer(t_sum.at[it]), t_dst.at[it], t_send.at[it], t_recv.at[it])
+            pair = t[:, p * width : (p + 1) * width] + t_half[it, p]
+            if it == 0:
+                t_sum16[p] = pair.astype(jnp.bfloat16)
+            else:
+                t_sum[it - 1, p] = pair
+        sent = t_sum16 if it == 0 else t_sum.at[it - 1]
+        arrived = t_dst16 if it == 0 else t_dst.at[it - 1]
+        t_args = (per_peer(sent), arrived, t_send.at[it], t_recv.at[it])
         start_chips(*t_args)
 
         wait_all(*gr_args)
@@ -301,10 +317,10 @@
         lower = inverse_factor(gfull[...] * (1.0 / sample_count), False)
 
         wait_chips(*t_args)
-        t_dst[it, chip] = t_sum[it, chip]
-        chunk = t_dst[it, 0]
+        arrived[chip] = sent[chip]
+        chunk = arrived[0].astype(jnp.float32)
         for p in range(1, chips):
-            chunk = chunk + t_dst[it, p]
+            chunk = chunk + arrived[p].astype(jnp.float32)
         z = dot32(lower, chunk)
         if it == ITERS:
             z = z * (1.0 / math.sqrt(sample_count))
@@ -333,13 +349,14 @@
             for p in range(chips):
                 zt[which, :, p * width : (p + 1) * width] = zg[it, which, p]
             zz = zt[which]
-            return dot16(zz, zz, NT), dot16(zz, x_ref[:, half_of(which)], NT)
+            turned = zz.astype(jnp.float32).T.astype(jnp.bfloat16)
+            return dot16(zz, zz, NT), dot16(x_ref[:, half_of(which)], turned, NN)
 
         gz_own, v_own = use_half(core)
         landed.wait()
         gz_far, v_far = use_half(1 - core)
         gz_done = snp_sum(gz_own + gz_far, gsl.at[it], gz_send.at[it], gz_recv.at[it])
-        v_done = snp_sum(v_own + v_far, ysl.at[it + 1], y_send.at[it + 1], y_recv.at[it + 1])
+        v_done = snp_sum((v_own + v_far).T, ysl.at[it], y_send.at[it + 1], y_recv.at[it + 1])
         upper = inverse_factor(gz_done() * (1.0 / snp_count), True)
         y = dot32(upper, v_done())
 
@@ -384,7 +401,8 @@
     a2 = lax.reduce_precision(weighted - a1, 8, 7)
     a3 = lax.reduce_precision(weighted - a1 - a2, 8, 7)
     lw = jnp.concatenate([a1, a1, a2, a1, a2, a3], axis=1).astype(jnp.bfloat16)
-    right_t = jnp.pad(right_factors.T, ((0, depth - rank), (0, 0)))
+    held = -(-rank // 8) * 8
+    right_t = jnp.pad(right_factors.T, ((0, held - rank), (0, 0)))
 
     f32, b16 = jnp.float32, jnp.bfloat16
     vm = pl.BlockSpec(memory_space=pltpu.VMEM)
@@ -409,14 +427,17 @@
         scratch_shapes=[
             pltpu.VMEM((rows, cols), jnp.int32),
             pltpu.VMEM((rows, cols), b16),
-            pltpu.VMEM((n, depth, width), f32),
+            pltpu.VMEM((2, n // 2, held, width), f32),
             pltpu.VMEM((6 * depth, cols), b16),
-            pltpu.VMEM((loops, m, k, rows), f32),
+            pltpu.VMEM((m, k, rows), b16),
+            pltpu.VMEM((ITERS, m, k, rows), f32),
             pltpu.VMEM((ITERS, m, k, k), f32),
             pltpu.VMEM((loops, n // 2, k, width), f32),
             pltpu.VMEM((loops, n // 2, k, width), f32),
-            pltpu.VMEM((loops, n // 2, k, width), f32),
-            pltpu.VMEM((loops, n // 2, k, width), f32),
+            pltpu.VMEM((ITERS, n // 2, k, width), f32),
+            pltpu.VMEM((ITERS, n // 2, k, width), f32),
+            pltpu.VMEM((n // 2, k, width), b16),
+            pltpu.VMEM((n // 2, k, width), b16),
             pltpu.VMEM((loops, n, piece, k), f32),
             pltpu.VMEM((loops, n, piece, k), f32),
             pltpu.VMEM((loops, piece, k), f32),
@@ -425,8 +446,10 @@
             pltpu.VMEM((loops, 2, n // 2, k, width), b16),
             pltpu.VMEM((2, k, cols // 2), b16),
             dma((rows // ROW_STEP,)),
-            dma((n,)),
-            dma((n,)),
+            dma((n // 2,)),
+            dma((n // 2,)),
+            dma,
+            dma,
             dma((loops, m)),
             dma((loops, m)),
             dma((ITERS, m)),

time: 109 us -> 105 us (0.963)
  Pallas kernels: 97.3 us -> 93.8 us
    pallas_call x1, Pallas kernels: 97.3 us -> 93.8 us  [on_device(): pl.pallas_call(functools.partial(kernel, n, m, float(rows * n), float(col...]
where the time goes in v3:
time: 105 us
  Pallas kernels  93.8 us (89%)
  local copies, waits for them, and re-layouts  6.35 us (6%)
  other arithmetic  3.61 us (3%)
    pallas_call x1, Pallas kernels, on_device(): pl.pallas_call(functools.partial(kernel, n, m, float(rows * n), float(col...  93.8 us
    unnamed x7, local copies, waits for them, and re-layouts  5.17 us

profile of v3, /device:TPU:0, one launch (start us, length us, event | category | flops | bytes accessed | tf_op | source)
XLA Modules:
  0.0 104.7 jit_solution(17003310510599961999)
XLA Ops:
  0.6 0.7 broadcast_subtract_fusion
  1.3 0.8 select_reduce_fusion.2
  2.1 0.7 sub.18
  2.7 0.7 select_reduce_fusion.1
  3.5 0.7 pad.9.right_ref
  4.2 0.3 fusion.2.mask_ref
  4.5 1.0 copy.16
  5.5 0.7 broadcast_multiply_fusion
  6.2 0.1 fusion.1
  6.3 0.5 concatenate.4.lw_ref
  6.7 1.2 %copy.18.sketch_ref = bf16[2048,64]{1,0:T(8,128)(2,1)S(1)} copy(bf16[2048,64]{0,1:T(8,128)(2,1)} %param.14) | data formatting | bytes 524288 | tf_op args[5]
  8.0 0.0 copy-start
  8.0 0.7 copy-done
  8.7 93.8 %shard_map.112 = (f32[64,640]{1,0:T(8,128)S(1)}, f32[64,2048]{1,0:T(8,128)S(1)}, f32[64,2048]{1,0:T(8,128)S(1)}) custom-call(s32[640,2048]{1,0:T(8,128)} %geno_ref.1, f32[1,2048]{1,0:T(1,128)S(1)} %bitcast.8, bf16[640,192]{1,0:T(8,128)(2,1)S(1)} %concatenate.4.lw_ref, f32[24,128]{1,0:T(8,128)S(1)} %pad.9.right_ref, bf16[2048,64]{1,0:T(8,128)(2,1)S(1)} %copy.18.sketch_ref, ...), custom_call_target="tpu_custom_call" | custom-call | flops 1006632960 | bytes 5242880 | tf_op jit(solution)/shard_map/pallas_call | solution.py:412
  102.5 0.7 copy.22
  103.1 0.8 copy.23
  103.9 0.8 copy.24
  (1 shorter events, 0.0 us)
Async XLA Ops:
  8.0 0.7 copy-start

commit v4 on v3

--- a/solution.py
+++ b/solution.py
@@ -52,13 +52,18 @@
         columns = [
             jnp.broadcast_to(a[:, base + j : base + j + 1], (count, 2 * k)) for j in group
         ]
-        for i, j in enumerate(group):
-            after = local < j if reverse else local > j
-            scale = 1.0 / columns[i][j : j + 1, :]
-            factor = jnp.where(after, columns[i] * scale, 0.0)
-            for later in range(i + 1, GROUP):
-                columns[later] = columns[later] - factor * columns[later][j : j + 1, :]
-            a = a - factor * a[j : j + 1, :]
+        for i in range(0, GROUP, 2):
+            j1, j2 = group[i], group[i + 1]
+            one, two = columns[i], columns[i + 1]
+            p, q, r = one[j1 : j1 + 1, :], two[j1 : j1 + 1, :], two[j2 : j2 + 1, :]
+            scale = 1.0 / (p * r - q * q)
+            after = local < j2 if reverse else local > j2
+            f1 = jnp.where(after, (one * r - two * q) * scale, 0.0)
+            f2 = jnp.where(after, (two * p - one * q) * scale, 0.0)
+            for later in range(i + 2, GROUP):
+                c = columns[later]
+                columns[later] = c - (f1 * c[j1 : j1 + 1, :] + f2 * c[j2 : j2 + 1, :])
+            a = a - (f1 * a[j1 : j1 + 1, :] + f2 * a[j2 : j2 + 1, :])
         if reverse:
             done.insert(0, a[count - GROUP :])
             a = a[: count - GROUP]
@@ -66,6 +71,12 @@
             done.append(a[:GROUP])
             a = a[GROUP:]
     a = jnp.concatenate(done, axis=0)
+    shift, near = (k - 1, rows + 1) if reverse else (1, rows - 1)
+    second = lax.rem(rows, 2) == (0 if reverse else 1)
+    partner = pltpu.roll(a, shift, 0)
+    cross = jnp.sum(jnp.where(lanes == near, a, 0.0), axis=1, keepdims=True)
+    pivot = jnp.sum(jnp.where(lanes == near, partner, 0.0), axis=1, keepdims=True)
+    a = jnp.where(second, a - (cross / pivot) * partner, a)
     diag = jnp.sum(jnp.where(lanes == rows, a, 0.0), axis=1, keepdims=True)
     return a[:, k:] * lax.rsqrt(diag)
 
@@ -77,14 +88,26 @@
     snp_count,
     geno_ref,
     freqs_ref,
-    lw_ref,
+    left_ref,
     right_ref,
     sketch_ref,
-    mask_ref,
+    singular_ref,
+    sizes_ref,
+    batch_ref,
+    block_ref,
     basis_ref,
     proj_ref,
     snpb_ref,
     geno,
+    freqs,
+    left,
+    right,
+    turned_sketch,
+    left_pad,
+    right_pad,
+    sketch,
+    lw,
+    mask,
     x_ref,
     rg,
     rt,
@@ -105,6 +128,7 @@
     zg,
     zt,
     geno_sem,
+    small_sem,
     rg_send,
     rg_recv,
     rh_send,
@@ -129,7 +153,8 @@
     me = lax.axis_index("samp")
     my = lax.axis_index("snp")
     rows, cols = x_ref.shape
-    k = sketch_ref.shape[1]
+    k = sketch_ref.shape[0]
+    rank, depth = left_ref.shape[0], left_pad.shape[0]
     width = cols // n
     steps = rows // ROW_STEP
     chips = n // 2
@@ -145,6 +170,19 @@
         at = pl.ds(i * ROW_STEP, ROW_STEP)
         return pltpu.make_async_copy(geno_ref.at[at], geno.at[at], geno_sem.at[i])
 
+    small = [
+        pltpu.make_async_copy(src, dst, small_sem.at[i])
+        for i, (src, dst) in enumerate(
+            (
+                (right_ref, right),
+                (left_ref, left),
+                (sketch_ref, turned_sketch),
+                (freqs_ref, freqs),
+            )
+        )
+    ]
+    for copy in small:
+        copy.start()
     for i in range(steps):
         geno_copy(i).start()
 
@@ -164,6 +202,10 @@
 
     lax.fori_loop(1, n, greet_samp, 0)
     lax.fori_loop(1, m, greet_snp, 0)
+    for copy in small:
+        copy.wait()
+    right_pad[...] = jnp.zeros_like(right_pad)
+    right_pad[:rank, :] = right[...]
     pl.semaphore_wait(barrier, n + m - 2)
 
     def remote(src, dst, send, recv, axis, peer):
@@ -216,16 +258,44 @@
     def per_peer(ref):
         return lambda peer: ref.at[peer]
 
-    rg_args = (one(right_ref), rg.at[core], rg_send, rg_recv)
+    rg_args = (one(right_pad), rg.at[core], rg_send, rg_recv)
     start_chips(*rg_args)
-    rg[core, chip] = right_ref[...]
-    depth = rt.shape[0] // 6
+    rg[core, chip] = right_pad[...]
+
+    row_at = lax.broadcasted_iota(jnp.int32, (16, 128), 0)
+    lane_at = lax.broadcasted_iota(jnp.int32, (16, 128), 1)
+    first_block = my * (cols // BLOCK)
+    table = jnp.zeros((16, 128), jnp.float32)
+    for j in range(batch_ref.shape[0]):
+        hit = (row_at == batch_ref[j]) & (lane_at == block_ref[j] - first_block)
+        table = jnp.where(hit, 1.0, table)
+    ids = me * rows + lax.broadcasted_iota(jnp.int32, (rows, 128), 0)
+    gone_rows = jnp.zeros((rows, 128), jnp.float32)
+    end = jnp.int32(0)
+    for b in range(BATCHES):
+        begin, end = end, end + sizes_ref[b]
+        inside = (ids >= begin) & (ids < end)
+        gone_rows = jnp.where(inside, table[b : b + 1, :], gone_rows)
+    mask[...] = gone_rows
+
+    left_pad[...] = jnp.zeros_like(left_pad)
+    left_pad[:rank, :] = left[...]
+    rank_at = lax.broadcasted_iota(jnp.int32, (depth, 128), 0)
+    scales = jnp.zeros((depth, 128), jnp.float32)
+    for j in range(rank):
+        scales = jnp.where(rank_at == j, singular_ref[j], scales)
+    weighted = left_pad[...] * scales[:, :1]
+    l1 = weighted.astype(jnp.bfloat16).astype(jnp.float32)
+    l2 = (weighted - l1).astype(jnp.bfloat16).astype(jnp.float32)
+    l3 = weighted - l1 - l2
+    lw[...] = jnp.concatenate([l1, l1, l2, l1, l2, l3], axis=0).T.astype(jnp.bfloat16)
+    sketch[...] = turned_sketch[...].astype(jnp.float32).T.astype(jnp.bfloat16)
     wait_chips(*rg_args)
     across = remote(rg.at[core], rg.at[core], rh_send, rh_recv, "samp", sibling)
     across.start()
     landed = remote(rg.at[core], rg.at[1 - core], rh_send, rh_recv, "samp", sibling)
     landed.wait()
-    blank = jnp.zeros((depth - right_ref.shape[0], width), jnp.float32)
+    blank = jnp.zeros((depth - right_pad.shape[0], width), jnp.float32)
     for p in range(n):
         piece = jnp.concatenate([rg[p % 2, p // 2], blank], axis=0)
         b1 = piece.astype(jnp.bfloat16)
@@ -240,9 +310,9 @@
         at = pl.ds(pl.multiple_of(i * ROW_STEP, ROW_STEP), ROW_STEP)
         for b in range(cols // BLOCK):
             cut = slice(b * BLOCK, (b + 1) * BLOCK)
-            lowrank = dot16(lw_ref[at, :], rt[:, cut], NN)
-            observed = geno[at, cut].astype(jnp.float32) - 2.0 * freqs_ref[:, cut]
-            gone = mask_ref[at, b : b + 1] > 0.5
+            lowrank = dot16(lw[at, :], rt[:, cut], NN)
+            observed = geno[at, cut].astype(jnp.float32) - 2.0 * freqs[:, cut]
+            gone = mask[at, b : b + 1] > 0.5
             x_ref[at, cut] = jnp.where(gone, lowrank, observed).astype(jnp.bfloat16)
         return c
 
@@ -262,7 +332,7 @@
 
         return finish
 
-    first = dot16(x_ref[...], sketch_ref[...], NN).T.astype(jnp.bfloat16)
+    first = dot16(x_ref[...], sketch[...], NN).T.astype(jnp.bfloat16)
     y = snp_sum(first, yfirst, y_send.at[0], y_recv.at[0])()
     piece_rows = k // n
     for it in range(ITERS + 1):
@@ -287,6 +357,15 @@
         )
         across.start()
         t = sketch_half(core)
+        wait_all(*gr_args)
+        gr_dst[it, me] = gr_src[it, me]
+        piece = gr_dst[it, 0]
+        for p in range(1, n):
+            piece = piece + gr_dst[it, p]
+        ga_src[it] = piece
+        ga_args = ("samp", n, me, one(ga_src.at[it]), ga_dst.at[it], ga_send.at[it], ga_recv.at[it])
+        start_all(*ga_args)
+        ga_dst[it, me] = piece
         across.wait()
         for p in range(chips):
             pair = t[:, p * width : (p + 1) * width] + t_half[it, p]
@@ -299,15 +378,6 @@
         t_args = (per_peer(sent), arrived, t_send.at[it], t_recv.at[it])
         start_chips(*t_args)
 
-        wait_all(*gr_args)
-        gr_dst[it, me] = gr_src[it, me]
-        piece = gr_dst[it, 0]
-        for p in range(1, n):
-            piece = piece + gr_dst[it, p]
-        ga_src[it] = piece
-        ga_args = ("samp", n, me, one(ga_src.at[it]), ga_dst.at[it], ga_send.at[it], ga_recv.at[it])
-        start_all(*ga_args)
-        ga_dst[it, me] = piece
         if it == ITERS:
             for c in range(2):
                 snpb_ref[:, c * half : (c + 1) * half] = dot32(upper, zt[c].astype(jnp.float32))
@@ -379,31 +449,7 @@
     rank = left_factors.shape[1]
     depth = -(-rank // 32) * 32
     width = cols // n
-    batch_range = jnp.arange(BATCHES, dtype=jnp.int32)
-    upto = batch_range[:, None] >= batch_range[None, :]
-    ends = jnp.sum(jnp.where(upto, batch_sizes[None, :], 0), axis=1)
-    begins = ends - batch_sizes
-    hot = missing_batch[:, None] == batch_range[None, :]
-    first = jnp.sum(jnp.where(hot, begins[None, :], 0), axis=1)
-    last = jnp.sum(jnp.where(hot, ends[None, :], 0), axis=1)
-    row_ids = lax.axis_index("samp") * rows + jnp.arange(rows, dtype=jnp.int32)
-    inside = (row_ids[:, None] >= first[None, :]) & (row_ids[:, None] < last[None, :])
-    local_block = missing_block - lax.axis_index("snp") * (cols // BLOCK)
-    hot_block = local_block[:, None] == jnp.arange(128, dtype=jnp.int32)[None, :]
-    mask = jnp.dot(
-        inside.astype(jnp.bfloat16),
-        hot_block.astype(jnp.bfloat16),
-        preferred_element_type=jnp.float32,
-    )
-
-    weighted = jnp.pad(left_factors * singular[None, :], ((0, 0), (0, depth - rank)))
-    a1 = lax.reduce_precision(weighted, 8, 7)
-    a2 = lax.reduce_precision(weighted - a1, 8, 7)
-    a3 = lax.reduce_precision(weighted - a1 - a2, 8, 7)
-    lw = jnp.concatenate([a1, a1, a2, a1, a2, a3], axis=1).astype(jnp.bfloat16)
     held = -(-rank // 8) * 8
-    right_t = jnp.pad(right_factors.T, ((0, held - rank), (0, 0)))
-
     f32, b16 = jnp.float32, jnp.bfloat16
     vm = pl.BlockSpec(memory_space=pltpu.VMEM)
     dma = pltpu.SemaphoreType.DMA
@@ -422,10 +468,20 @@
             jax.ShapeDtypeStruct((k, cols), f32),
             jax.ShapeDtypeStruct((k, cols), f32),
         ),
-        in_specs=[pl.BlockSpec(memory_space=pl.ANY)] + [vm] * 5,
+        in_specs=[pl.BlockSpec(memory_space=pl.ANY)] * 5
+        + [pl.BlockSpec(memory_space=pltpu.SMEM)] * 4,
         out_specs=(vm, vm, vm),
         scratch_shapes=[
             pltpu.VMEM((rows, cols), jnp.int32),
+            pltpu.VMEM((1, cols), f32),
+            pltpu.VMEM((rank, rows), f32),
+            pltpu.VMEM((rank, width), f32),
+            pltpu.VMEM((k, cols), b16),
+            pltpu.VMEM((depth, rows), f32),
+            pltpu.VMEM((held, width), f32),
+            pltpu.VMEM((cols, k), b16),
+            pltpu.VMEM((rows, 6 * depth), b16),
+            pltpu.VMEM((rows, 128), f32),
             pltpu.VMEM((rows, cols), b16),
             pltpu.VMEM((2, n // 2, held, width), f32),
             pltpu.VMEM((6 * depth, cols), b16),
@@ -446,6 +502,7 @@
             pltpu.VMEM((loops, 2, n // 2, k, width), b16),
             pltpu.VMEM((2, k, cols // 2), b16),
             dma((rows // ROW_STEP,)),
+            dma((4,)),
             dma((n // 2,)),
             dma((n // 2,)),
             dma,
@@ -473,7 +530,17 @@
         cost_estimate=pl.CostEstimate(
             flops=12 * rows * cols * k, bytes_accessed=4 * rows * cols, transcendentals=0
         ),
-    )(genotype, freqs[None, :], lw, right_t, sketch, mask)
+    )(
+        genotype,
+        freqs[None, :],
+        left_factors.T,
+        right_factors.T,
+        sketch.T,
+        singular,
+        batch_sizes,
+        missing_batch,
+        missing_block,
+    )
     return basis_t.T, proj_t.T, snpb_t.T
 
 

time: 105 us -> 103 us (0.981)
  other arithmetic: 3.61 us -> 0 us
  local copies, waits for them, and re-layouts: 6.35 us -> 8.05 us
    unnamed x7 -> x19, local copies, waits for them, and re-layouts: 5.17 us -> 8.05 us
    reduce_sum x2 -> x0, other arithmetic: 1.51 us -> none  [the longest x1 0.77 us: on_device(): ends = jnp.sum(jnp.where(upto, batch_sizes[None, :], 0), axis=1)]
    sub x2 -> x0, other arithmetic: 1.32 us -> none  [the longest x1 0.66 us: on_device(): begins = ends - batch_sizes]
where the time goes in v4:
time: 103 us; the launch traced here: 102 us
  Pallas kernels  93.7 us (91%)
  local copies, waits for them, and re-layouts  8.05 us (8%)
    pallas_call x1, Pallas kernels, on_device(): pl.pallas_call(functools.partial(kernel, n, m, float(rows * n), float(col...  93.7 us
    unnamed x19, local copies, waits for them, and re-layouts  8.05 us

profile of v4, /device:TPU:0, one launch (start us, length us, event | category | flops | bytes accessed | tf_op | source)
XLA Modules:
  0.0 102.4 jit_solution(191595667080125474)
XLA Ops:
  0.6 0.0 copy-start
  0.6 0.9 copy-done
  1.6 0.0 copy-start.1
  1.6 0.8 copy-done.1
  2.4 0.0 copy-start.2
  2.4 0.7 copy-done.2
  3.1 0.0 copy-start.3
  3.1 0.7 copy-done.3
  3.8 0.0 copy-start.4
  3.8 0.7 copy-done.4
  4.5 0.0 copy-start.5
  4.5 0.7 copy-done.5
  5.1 0.0 copy-start.6
  5.1 0.7 copy-done.6
  5.8 0.0 copy-start.7
  5.8 0.7 copy-done.7
  6.4 93.7 %shard_map.112 = (f32[64,640]{1,0:T(8,128)S(1)}, f32[64,2048]{1,0:T(8,128)S(1)}, f32[64,2048]{1,0:T(8,128)S(1)}) custom-call(s32[640,2048]{1,0:T(8,128)} %geno_ref.1, f32[1,2048]{1,0:T(1,128)S(1)} %bitcast.13, f32[20,640]{1,0:T(8,128)S(1)} %bitcast.11, f32[20,128]{1,0:T(8,128)S(1)} %bitcast.12, bf16[64,2048]{1,0:T(8,128)(2,1)S(1)} %bitcast.9, ...), custom_call_target="tpu_custom_call" | custom-call | flops 1006632960 | bytes 5242880 | tf_op jit(solution)/shard_map/pallas_call | solution.py:458
  100.1 0.7 copy.15
  100.8 0.8 copy.16
  101.6 0.8 copy.17
Async XLA Ops:
  0.6 1.0 copy-start
  1.6 0.8 copy-start.1
  2.4 0.7 copy-start.2
  3.1 0.7 copy-start.3
  3.8 0.7 copy-start.4
  4.5 0.7 copy-start.5
  5.1 0.7 copy-start.6
  5.8 0.7 copy-start.7

commit v5 on v4

--- a/solution.py
+++ b/solution.py
@@ -91,14 +91,18 @@
     left_ref,
     right_ref,
     sketch_ref,
+    singular_any,
+    sizes_any,
+    batch_any,
+    block_any,
+    basis_ref,
+    proj_ref,
+    snpb_ref,
+    geno,
     singular_ref,
     sizes_ref,
     batch_ref,
     block_ref,
-    basis_ref,
-    proj_ref,
-    snpb_ref,
-    geno,
     freqs,
     left,
     right,
@@ -120,11 +124,9 @@
     t_dst,
     t_sum16,
     t_dst16,
-    gr_src,
-    gr_dst,
-    ga_src,
-    ga_dst,
-    gfull,
+    g_src,
+    g_half,
+    g_all,
     zg,
     zt,
     geno_sem,
@@ -143,8 +145,8 @@
     t_recv,
     zh_send,
     zh_recv,
-    gr_send,
-    gr_recv,
+    gh_send,
+    gh_recv,
     ga_send,
     ga_recv,
     z_send,
@@ -178,6 +180,10 @@
                 (left_ref, left),
                 (sketch_ref, turned_sketch),
                 (freqs_ref, freqs),
+                (singular_any, singular_ref),
+                (sizes_any, sizes_ref),
+                (batch_any, batch_ref),
+                (block_any, block_ref),
             )
         )
     ]
@@ -334,16 +340,16 @@
 
     first = dot16(x_ref[...], sketch[...], NN).T.astype(jnp.bfloat16)
     y = snp_sum(first, yfirst, y_send.at[0], y_recv.at[0])()
-    piece_rows = k // n
     for it in range(ITERS + 1):
         hi, lo = split2(y)
         both = jnp.concatenate([hi, lo], axis=0)
         g4 = dot16(both, both, NT)
         gram = g4[:k, :k] + (g4[:k, k:] + g4[k:, :k])
-        for p in range(n):
-            gr_src[it, p] = gram[p * piece_rows : (p + 1) * piece_rows]
-        gr_args = ("samp", n, me, per_peer(gr_src.at[it]), gr_dst.at[it], gr_send.at[it], gr_recv.at[it])
-        start_all(*gr_args)
+        g_src[it] = jnp.concatenate([gram[: k // 2], gram[k // 2 :]], axis=1)
+        g_across = remote(
+            g_src.at[it], g_half.at[it], gh_send.at[it], gh_recv.at[it], "samp", sibling
+        )
+        g_across.start()
 
         def sketch_half(which):
             t2 = dot16(both, x_ref[:, half_of(which)], NN)
@@ -356,16 +362,11 @@
             t_src.at[it], t_half.at[it], h_send.at[it], h_recv.at[it], "samp", sibling
         )
         across.start()
+        g_across.wait()
+        g_all[it, chip] = g_src[it] + g_half[it]
+        g_args = (one(g_all.at[it, chip]), g_all.at[it], ga_send.at[it], ga_recv.at[it])
+        start_chips(*g_args)
         t = sketch_half(core)
-        wait_all(*gr_args)
-        gr_dst[it, me] = gr_src[it, me]
-        piece = gr_dst[it, 0]
-        for p in range(1, n):
-            piece = piece + gr_dst[it, p]
-        ga_src[it] = piece
-        ga_args = ("samp", n, me, one(ga_src.at[it]), ga_dst.at[it], ga_send.at[it], ga_recv.at[it])
-        start_all(*ga_args)
-        ga_dst[it, me] = piece
         across.wait()
         for p in range(chips):
             pair = t[:, p * width : (p + 1) * width] + t_half[it, p]
@@ -381,10 +382,12 @@
         if it == ITERS:
             for c in range(2):
                 snpb_ref[:, c * half : (c + 1) * half] = dot32(upper, zt[c].astype(jnp.float32))
-        wait_all(*ga_args)
-        for p in range(n):
-            gfull[p * piece_rows : (p + 1) * piece_rows, :] = ga_dst[it, p]
-        lower = inverse_factor(gfull[...] * (1.0 / sample_count), False)
+        wait_chips(*g_args)
+        packed = g_all[it, 0]
+        for p in range(1, chips):
+            packed = packed + g_all[it, p]
+        gram = jnp.concatenate([packed[:, :k], packed[:, k:]], axis=0)
+        lower = inverse_factor(gram * (1.0 / sample_count), False)
 
         wait_chips(*t_args)
         arrived[chip] = sent[chip]
@@ -454,7 +457,6 @@
     vm = pl.BlockSpec(memory_space=pltpu.VMEM)
     dma = pltpu.SemaphoreType.DMA
     loops = ITERS + 1
-    piece = k // n
     basis_t, proj_t, snpb_t = pl.pallas_call(
         functools.partial(
             kernel,
@@ -468,11 +470,14 @@
             jax.ShapeDtypeStruct((k, cols), f32),
             jax.ShapeDtypeStruct((k, cols), f32),
         ),
-        in_specs=[pl.BlockSpec(memory_space=pl.ANY)] * 5
-        + [pl.BlockSpec(memory_space=pltpu.SMEM)] * 4,
+        in_specs=[pl.BlockSpec(memory_space=pl.ANY)] * 9,
         out_specs=(vm, vm, vm),
         scratch_shapes=[
             pltpu.VMEM((rows, cols), jnp.int32),
+            pltpu.SMEM(singular.shape, f32),
+            pltpu.SMEM(batch_sizes.shape, jnp.int32),
+            pltpu.SMEM(missing_batch.shape, jnp.int32),
+            pltpu.SMEM(missing_block.shape, jnp.int32),
             pltpu.VMEM((1, cols), f32),
             pltpu.VMEM((rank, rows), f32),
             pltpu.VMEM((rank, width), f32),
@@ -494,15 +499,13 @@
             pltpu.VMEM((ITERS, n // 2, k, width), f32),
             pltpu.VMEM((n // 2, k, width), b16),
             pltpu.VMEM((n // 2, k, width), b16),
-            pltpu.VMEM((loops, n, piece, k), f32),
-            pltpu.VMEM((loops, n, piece, k), f32),
-            pltpu.VMEM((loops, piece, k), f32),
-            pltpu.VMEM((loops, n, piece, k), f32),
-            pltpu.VMEM((k, k), f32),
+            pltpu.VMEM((loops, k // 2, 2 * k), f32),
+            pltpu.VMEM((loops, k // 2, 2 * k), f32),
+            pltpu.VMEM((loops, n // 2, k // 2, 2 * k), f32),
             pltpu.VMEM((loops, 2, n // 2, k, width), b16),
             pltpu.VMEM((2, k, cols // 2), b16),
             dma((rows // ROW_STEP,)),
-            dma((4,)),
+            dma((8,)),
             dma((n // 2,)),
             dma((n // 2,)),
             dma,
@@ -517,15 +520,15 @@
             dma((loops, n // 2)),
             dma((loops,)),
             dma((loops,)),
-            dma((loops, n)),
-            dma((loops, n)),
-            dma((loops, n)),
-            dma((loops, n)),
+            dma((loops,)),
+            dma((loops,)),
+            dma((loops, n // 2)),
+            dma((loops, n // 2)),
             dma((loops, n // 2)),
             dma((loops, n // 2)),
         ],
         compiler_params=pltpu.CompilerParams(
-            collective_id=0, has_side_effects=True, vmem_limit_bytes=48 * 1024 * 1024
+            collective_id=0, has_side_effects=True, vmem_limit_bytes=62 * 1024 * 1024
         ),
         cost_estimate=pl.CostEstimate(
             flops=12 * rows * cols * k, bytes_accessed=4 * rows * cols, transcendentals=0

time: 103 us -> 95.9 us (0.931)
  Pallas kernels: 93.7 us -> 89.7 us
  local copies, waits for them, and re-layouts: 8.05 us -> 5.34 us
    pallas_call x1, Pallas kernels: 93.7 us -> 89.7 us  [on_device(): pl.pallas_call(functools.partial(kernel, n, m, float(rows * n), float(col...]
    unnamed x19 -> x3, local copies, waits for them, and re-layouts: 8.05 us -> 5.34 us
where the time goes in v5:
time: 95.9 us; the launch traced here: 95.7 us
  Pallas kernels  89.7 us (94%)
  local copies, waits for them, and re-layouts  5.34 us (6%)
    pallas_call x1, Pallas kernels, on_device(): pl.pallas_call(functools.partial(kernel, n, m, float(rows * n), float(col...  89.7 us
    unnamed x3, local copies, waits for them, and re-layouts  5.34 us

profile of v5, /device:TPU:0, one launch (start us, length us, event | category | flops | bytes accessed | tf_op | source)
XLA Modules:
  0.0 95.7 jit_solution(1984794486806064746)
XLA Ops:
  0.6 89.7 %shard_map.112 = (f32[64,640]{1,0:T(8,128)}, f32[64,2048]{1,0:T(8,128)}, f32[64,2048]{1,0:T(8,128)}) custom-call(s32[640,2048]{1,0:T(8,128)} %geno_ref.1, f32[1,2048]{1,0:T(1,128)} %bitcast.13, f32[20,640]{1,0:T(8,128)} %bitcast.11, f32[20,128]{1,0:T(8,128)} %bitcast.12, bf16[64,2048]{1,0:T(8,128)(2,1)} %bitcast.9, f32[20]{0:T(128)} %singular_any.1, ...), custom_call_target="tpu_custom_call" | custom-call | flops 1006632960 | bytes 5242880 | tf_op jit(solution)/shard_map/pallas_call | solution.py:460
  90.3 1.6 %copy.15 = f32[640,64]{0,1:T(8,128)} copy(f32[640,64]{0,1:T(8,128)} %bitcast.10) | data formatting | bytes 327680
  91.9 1.9 %copy.16 = f32[2048,64]{0,1:T(8,128)} copy(f32[2048,64]{0,1:T(8,128)} %bitcast.8) | data formatting | bytes 1048576
  93.8 1.9 %copy.17 = f32[2048,64]{0,1:T(8,128)} copy(f32[2048,64]{0,1:T(8,128)} %bitcast.7) | data formatting | bytes 1048576

commit v6 on v5

--- a/solution.py
+++ b/solution.py
@@ -466,9 +466,9 @@
             float(cols * m),
         ),
         out_shape=(
-            jax.ShapeDtypeStruct((k, rows), f32),
-            jax.ShapeDtypeStruct((k, cols), f32),
-            jax.ShapeDtypeStruct((k, cols), f32),
+            pltpu.VMEM((k, rows), f32),
+            pltpu.VMEM((k, cols), f32),
+            pltpu.VMEM((k, cols), f32),
         ),
         in_specs=[pl.BlockSpec(memory_space=pl.ANY)] * 9,
         out_specs=(vm, vm, vm),
@@ -528,7 +528,7 @@
             dma((loops, n // 2)),
         ],
         compiler_params=pltpu.CompilerParams(
-            collective_id=0, has_side_effects=True, vmem_limit_bytes=62 * 1024 * 1024
+            collective_id=0, has_side_effects=True, vmem_limit_bytes=60 * 1024 * 1024
         ),
         cost_estimate=pl.CostEstimate(
             flops=12 * rows * cols * k, bytes_accessed=4 * rows * cols, transcendentals=0

time: 95.9 us -> 91.8 us (0.957)
  local copies, waits for them, and re-layouts: 5.34 us -> 2.25 us
  Pallas kernels: 89.7 us -> 88.7 us
    unnamed x3, local copies, waits for them, and re-layouts: 5.34 us -> 2.25 us
    pallas_call x1, Pallas kernels: 89.7 us -> 88.7 us  [on_device(): pl.pallas_call(functools.partial(kernel, n, m, float(rows * n), float(col...]
where the time goes in v6:
time: 91.8 us; the launch traced here: 91.6 us
  Pallas kernels  88.7 us (97%)
  local copies, waits for them, and re-layouts  2.25 us (2%)
    pallas_call x1, Pallas kernels, on_device(): pl.pallas_call(functools.partial(kernel, n, m, float(rows * n), float(col...  88.7 us
    unnamed x3, local copies, waits for them, and re-layouts  2.25 us

profile of v6, /device:TPU:0, one launch (start us, length us, event | category | flops | bytes accessed | tf_op | source)
XLA Modules:
  0.0 91.6 jit_solution(14973017216473073763)
XLA Ops:
  0.6 88.7 %shard_map.112 = (f32[64,640]{1,0:T(8,128)S(1)}, f32[64,2048]{1,0:T(8,128)S(1)}, f32[64,2048]{1,0:T(8,128)S(1)}) custom-call(s32[640,2048]{1,0:T(8,128)} %geno_ref.1, f32[1,2048]{1,0:T(1,128)} %bitcast.13, f32[20,640]{1,0:T(8,128)} %bitcast.11, f32[20,128]{1,0:T(8,128)} %bitcast.12, bf16[64,2048]{1,0:T(8,128)(2,1)} %bitcast.10, f32[20]{0:T(128)} %singular_any.1, ...), custom_call_target="tpu_custom_call" | custom-call | flops 1006632960 | bytes 5242880 | tf_op jit(solution)/shard_map/pallas_call | solution.py:460
  89.3 0.7 copy.15
  90.0 0.8 copy.16
  90.8 0.8 copy.17
